TPU v7x, 32 devices: a whole 2x2x4 slice. The times are simulated.
32 devices in a mesh: groups: 1, node: 4 (over y, x), ep: 8 (over z, core).
Axes of the slice: x: 2, y: 2, z: 4, core: 2. Of those that a mesh axis runs over, the one named last changes fastest.
Arguments:
- tokens: bfloat16 [2048, 4096], P(('groups', 'node', 'ep')), may hold values from -6 to 6
- expert_ids: int32 [2048, 8], P(('groups', 'node', 'ep')), may hold values from 0 to 15, all different within a row; in each aligned block of 64 rows (0 to 63, 64 to 127, ...) at most 48 rows name the same one
- gate_values: float32 [2048, 8], P(('groups', 'node', 'ep')), may hold values from 0.1 to 1
- gate_weight: bfloat16 [32, 2048, 768], P(('node', 'ep')), may hold values from -0.09375 to 0.09375
- up_weight: bfloat16 [32, 2048, 768], P(('node', 'ep')), may hold values from -0.09375 to 0.09375
- down_weight: bfloat16 [32, 768, 2048], P(('node', 'ep')), may hold values from -0.21875 to 0.21875
Outputs:
- mixed: bfloat16 [2048, 4096], P(('groups', 'node', 'ep'))
Inputs may be any that keep to these rules, and one draw needn't show every extreme that they name: `expert_ids`: each row names 8 different experts. In the 64 rows of one device no expert is named more than 48 times, and in every draw some device names some expert exactly 48 times.
All inputs are finite; a program needn't handle non-finite values.
Results may differ from a plain program's by a relative error of at most 0.017.
Values may be sent and summed in bfloat16 or wider, within the bound.
A program may use at most 128 MiB of HBM per device.

v0:
```python
import jax
import jax.numpy as jnp
from jax import lax
from jax.sharding import PartitionSpec as P


def partner(array, axis, stride):
    return lax.ppermute(array, axis, [(i, i ^ 1 << stride) for i in range(lax.axis_size(axis))])


def quantize(tokens):
    row_count, model_width = tokens.shape
    scaled = tokens.astype(jnp.float32).reshape(row_count, model_width // 128, 128)
    largest = jnp.max(jnp.abs(scaled), axis=2)
    block_scales = ((largest + 1e-06) / 448.0).astype(jnp.bfloat16)
    quantized = (scaled / block_scales.astype(jnp.float32)[:, :, None]).astype(jnp.bfloat16)
    return (quantized.reshape(row_count, model_width), block_scales)


def slot_positions(flat_ids, expert_count):
    matches = (flat_ids[..., None] == jnp.arange(expert_count, dtype=jnp.int32)).astype(jnp.int32)
    running = jnp.cumsum(matches, axis=-2)
    return jnp.sum(matches * running, axis=-1) - 1


def restore(pieces):
    quantized, block_scales = pieces
    leading = quantized.shape[:2]
    row_width = quantized.shape[2]
    block_count = block_scales.shape[2]
    scaled = quantized.astype(jnp.float32).reshape(
        leading + (block_count, row_width // block_count)
    )
    scaled = scaled * block_scales.astype(jnp.float32)[..., None]
    return (scaled.reshape(-1, row_width).astype(jnp.bfloat16), leading)


def expert_rows(pieces, gate_half, up_half, down_half):
    restored, leading = restore(pieces)
    gate_part = jnp.dot(restored, gate_half, preferred_element_type=jnp.float32)
    up_part = jnp.dot(restored, up_half, preferred_element_type=jnp.float32)
    gate_other, up_other = partner((gate_part, up_part), "ep", 0)
    gate_sum = gate_part + gate_other
    up_sum = up_part + up_other
    hidden = (jax.nn.silu(gate_sum) * up_sum).astype(jnp.bfloat16)
    result = jnp.dot(hidden, down_half, preferred_element_type=jnp.float32).astype(jnp.bfloat16)
    return result.reshape(leading + (down_half.shape[1],))


def on_device(tokens, expert_ids, gate_values, gate_weight, up_weight, down_weight):
    row_count, model_width = tokens.shape
    route_count = expert_ids.shape[1]
    half_width = model_width // 2
    node_count = lax.axis_size("node")
    owner_count = lax.axis_size("ep")
    device_count = node_count * owner_count
    expert_count = device_count // 2
    capacity = min(row_count, 3 * row_count * route_count // (2 * expert_count))
    quantized, block_scales = quantize(tokens)
    block_total = block_scales.shape[1]
    half_blocks = block_total // 2
    flat_ids = expert_ids.reshape(-1)
    positions_in = slot_positions(flat_ids, expert_count)
    route_total = row_count * route_count
    token_index = jnp.arange(route_total, dtype=jnp.int32) // route_count
    slot_table = jnp.full((expert_count * capacity,), row_count, jnp.int32)
    slot_table = slot_table.at[flat_ids * capacity + positions_in].set(token_index)
    half_index = jnp.arange(2, dtype=jnp.int32)
    quant_rows = jnp.concatenate(
        [
            quantized.reshape(row_count, 2, half_width).swapaxes(0, 1),
            jnp.zeros((2, 1, half_width), jnp.bfloat16),
        ],
        axis=1,
    ).reshape(2 * (row_count + 1), half_width)
    scale_rows = jnp.concatenate(
        [
            block_scales.reshape(row_count, 2, half_blocks).swapaxes(0, 1),
            jnp.zeros((2, 1, half_blocks), jnp.bfloat16),
        ],
        axis=1,
    ).reshape(2 * (row_count + 1), half_blocks)
    picked = (
        half_index[None, :, None] * (row_count + 1) + slot_table.reshape(expert_count, 1, capacity)
    ).reshape(device_count, capacity)
    sent_quant = quant_rows[picked]
    sent_scales = scale_rows[picked]
    outputs = expert_rows(
        (
            lax.all_to_all(sent_quant, ("node", "ep"), split_axis=0, concat_axis=0, tiled=True),
            lax.all_to_all(sent_scales, ("node", "ep"), split_axis=0, concat_axis=0, tiled=True),
        ),
        gate_weight[0],
        up_weight[0],
        down_weight[0],
    )
    returned = lax.all_to_all(outputs, ("node", "ep"), split_axis=0, concat_axis=0, tiled=True)
    paired = returned.reshape(expert_count, 2, capacity, half_width)
    gathered = paired[flat_ids, :, positions_in].reshape(route_total, model_width)
    weighted = gathered.astype(jnp.float32) * gate_values.reshape(-1)[:, None]
    mixed = jnp.sum(weighted.reshape(row_count, route_count, model_width), axis=1)
    return mixed.astype(jnp.bfloat16)


def solution(mesh):
    in_specs = (
        P(("groups", "node", "ep"), None),
        P(("groups", "node", "ep"), None),
        P(("groups", "node", "ep"), None),
        P(("node", "ep"), None, None),
        P(("node", "ep"), None, None),
        P(("node", "ep"), None, None),
    )
    out_specs = P(("groups", "node", "ep"), None)
    return jax.shard_map(
        on_device, mesh=mesh, in_specs=in_specs, out_specs=out_specs, check_vma=False
    )
```

profile of v0, /device:TPU:0, one launch (start us, length us, event | category | flops | bytes accessed | tf_op | source)
XLA Modules:
  0.0 428.8 jit_solution(12215663661034235551)
XLA Ops:
  0.0 0.9 copy.43
  1.2 1.2 reduce-window.6
  2.8 2.4 scatter_custom_fusion
  5.6 1.1 abs_bitcast_fusion
  6.7 1.2 copy.56
  7.9 1.6 reduce_max.9
  9.8 4.1 gather_fusion.1
  13.9 1.2 copy.49
  15.8 7.3 %all-to-all-start.1 = ((bf16[32,2,384]{2,1,0:T(2,128)(2,1)}), bf16[32,2,384]{2,1,0:T(2,128)(2,1)S(1)}, u32[]{:S(2)}, u32[]{:S(2)}) async-start(bf16[32,2,384]{2,1,0:T(2,128)(2,1)} %reshape.241), calls=%async_computation.1 | async-start | bytes 98304 | tf_op jit(solution)/shard_map/all_to_all | solution.py:91
  23.2 3.1 reshape.198
  26.3 1.3 div.31
  27.6 2.8 div.32
  30.4 2.4 fusion.6
  33.9 2.0 reshape.199
  35.8 13.9 %gather_fusion = bf16[1536,2048]{1,0:T(8,128)(2,1)} fusion(bf16[130,2048]{1,0:T(8,128)(2,1)} %reshape.199, s32[2048]{0:T(1024)S(1)} %pad_clamp_fusion), kind=kCustom, calls=%fused_computation | custom fusion | bytes 12589056 | tf_op jit(solution)/shard_map/gather | solution.py:86
  49.7 6.1 %all-to-all-start = ((bf16[32,48,2048]{2,1,0:T(8,128)(2,1)}), bf16[32,48,2048]{2,1,0:T(8,128)(2,1)}, u32[]{:S(2)}, u32[]{:S(2)}) async-start(bf16[32,48,2048]{2,1,0:T(8,128)(2,1)} %bitcast.53), calls=%async_computation | async-start | bytes 12582912 | tf_op jit(solution)/shard_map/all_to_all | solution.py:90
  56.0 1.1 copy.50
  57.1 8.4 %mul.53 = f32[32,48,16,128]{3,2,1,0:T(8,128)} broadcast(f32[32,48,16]{2,1,0:T(8,128)} %copy.50), dimensions={0,1,2} | broadcast | bytes 12681216 | tf_op jit(solution)/shard_map/mul | solution.py:34
  65.5 13.6 %mul.54 = f32[32,48,2048]{2,1,0:T(8,128)} reshape(f32[32,48,16,128]{3,2,1,0:T(8,128)} %mul.53) | data formatting | bytes 25165824 | tf_op jit(solution)/shard_map/mul | solution.py:34
  79.1 116.5 %all-to-all-done = bf16[32,48,2048]{2,1,0:T(8,128)(2,1)} async-done(((bf16[32,48,2048]{2,1,0:T(8,128)(2,1)}), bf16[32,48,2048]{2,1,0:T(8,128)(2,1)}, u32[]{:S(2)}, u32[]{:S(2)}) %all-to-all-start) | async-done | bytes 6291488 | tf_op jit(solution)/shard_map/all_to_all | solution.py:90
  195.6 11.6 %multiply_convert_fusion = bf16[32,48,2048]{2,1,0:T(8,128)(2,1)} fusion(f32[32,48,2048]{2,1,0:T(8,128)} %mul.54, bf16[32,48,2048]{2,1,0:T(8,128)(2,1)} %all-to-all-done), kind=kLoop, calls=%fused_computation.4 | loop fusion | flops 9437184 | bytes 25165824 | tf_op jit(solution)/shard_map/convert_element_type | solution.py:35
  207.3 8.2 %fusion.3 = f32[1536,768]{1,0:T(8,128)S(1)} fusion(bf16[1536,2048]{1,0:T(8,128)(2,1)} %bitcast.55, bf16[1,2048,768]{2,1,0:T(8,128)(2,1)} %param.9), kind=kOutput, calls=%fused_computation.11 | convolution fusion | flops 4831838208 | bytes 14155776 | tf_op jit(solution)/shard_map/dot_general | solution.py:40
  215.6 5.2 %fusion.1 = f32[1536,768]{1,0:T(8,128)S(1)} fusion(bf16[1536,2048]{1,0:T(8,128)(2,1)S(1)} %bitcast.56, bf16[1,2048,768]{2,1,0:T(8,128)(2,1)S(1)} %copy-done.3), kind=kOutput, calls=%fused_computation.9 | convolution fusion | flops 4831838208 | bytes 14155776 | tf_op jit(solution)/shard_map/dot_general | solution.py:41
  221.4 2.1 collective-permute-done
  223.5 6.9 %collective-permute-done.1 = f32[1536,768]{1,0:T(8,128)} collective-permute-done((f32[1536,768]{1,0:T(8,128)S(1)}, f32[1536,768]{1,0:T(8,128)}, u32[]{:S(2)}, u32[]{:S(2)}) %collective-permute-start.1) | collective-permute-done | bytes 4718624 | tf_op jit(solution)/shard_map/ppermute | solution.py:8
  230.4 10.6 %convolution_convert_fusion = bf16[1536,2048]{1,0:T(8,128)(2,1)} fusion(bf16[1,768,2048]{2,1,0:T(8,128)(2,1)S(1)} %copy-done, f32[1536,768]{1,0:T(8,128)S(1)} %fusion.1, f32[1536,768]{1,0:T(8,128)} %collective-permute-done.1, f32[1536,768]{1,0:T(8,128)S(1)} %fusion.3, f32[1536,768]{1,0:T(8,128)S(1)} %collective-permute-done), kind=kOutput, calls=%fused_computation.6 | convolution fusion | flops 4844421120 | bytes 28311552 | tf_op jit(solution)/shard_map/dot_general | solution.py:46
  240.9 3.7 all-to-all-start.2
  244.8 139.9 %all-to-all-done.2 = bf16[32,48,2048]{2,1,0:T(8,128)(2,1)} async-done(((bf16[32,48,2048]{2,1,0:T(8,128)(2,1)}), bf16[32,48,2048]{2,1,0:T(8,128)(2,1)}, u32[]{:S(2)}, u32[]{:S(2)}) %all-to-all-start.2) | async-done | bytes 6291488 | tf_op jit(solution)/shard_map/all_to_all | solution.py:97
  384.6 12.7 %copy.51 = bf16[16,2,48,2048]{3,1,2,0:T(2,128)(2,1)} copy(bf16[16,2,48,2048]{3,2,1,0:T(8,128)(2,1)} %bitcast.14) | data formatting | bytes 12582912 | tf_op jit(solution)/shard_map/reshape | solution.py:98
  397.4 16.2 %gather_fusion.2 = bf16[512,2,2048]{2,1,0:T(2,128)(2,1)} fusion(bf16[16,2,48,2048]{3,1,2,0:T(2,128)(2,1)} %copy.51, s32[512]{0:T(512)S(1)} %bitcast.52), kind=kCustom, calls=%fused_computation.2 | custom fusion | bytes 8392704 | tf_op jit(solution)/shard_map/gather | solution.py:99
  413.6 8.1 %reshape.205 = f32[64,8,4096]{2,1,0:T(8,128)} reshape(bf16[512,2,2048]{2,1,0:T(2,128)(2,1)} %gather_fusion.2) | data formatting | bytes 12582912 | tf_op jit(solution)/shard_map/convert_element_type | solution.py:100
  421.7 7.1 %multiply_reduce_fusion = bf16[64,4096]{1,0:T(8,128)(2,1)} fusion(f32[64,8,4096]{2,1,0:T(8,128)} %reshape.205, f32[64,8]{1,0:T(8,128)S(1)} %copy.52), kind=kLoop, calls=%fused_computation.5 | loop fusion | flops 3932160 | bytes 8914944 | tf_op jit(solution)/shard_map/reduce_sum | solution.py:101
  (42 shorter events, 4.1 us)
Async XLA Ops:
  0.0 230.4 %copy-start = (bf16[1,768,2048]{2,1,0:T(8,128)(2,1)S(1)}, bf16[1,768,2048]{2,1,0:T(8,128)(2,1)}, u32[]{:S(2)}) copy-start(bf16[1,768,2048]{2,1,0:T(8,128)(2,1)} %param.11) | copy-start | bytes 9437188
  15.8 33.9 %all-to-all-start.1 = ((bf16[32,2,384]{2,1,0:T(2,128)(2,1)}), bf16[32,2,384]{2,1,0:T(2,128)(2,1)S(1)}, u32[]{:S(2)}, u32[]{:S(2)}) async-start(bf16[32,2,384]{2,1,0:T(2,128)(2,1)} %reshape.241), calls=%async_computation.1 | async-start | bytes 98304 | tf_op jit(solution)/shard_map/all_to_all | solution.py:91
  49.7 145.9 %all-to-all-start = ((bf16[32,48,2048]{2,1,0:T(8,128)(2,1)}), bf16[32,48,2048]{2,1,0:T(8,128)(2,1)}, u32[]{:S(2)}, u32[]{:S(2)}) async-start(bf16[32,48,2048]{2,1,0:T(8,128)(2,1)} %bitcast.53), calls=%async_computation | async-start | bytes 12582912 | tf_op jit(solution)/shard_map/all_to_all | solution.py:90
  207.3 8.3 %copy-start.1 = (bf16[32,48,2048]{2,1,0:T(8,128)(2,1)S(1)}, bf16[32,48,2048]{2,1,0:T(8,128)(2,1)}, u32[]{:S(2)}) copy-start(bf16[32,48,2048]{2,1,0:T(8,128)(2,1)} %multiply_convert_fusion) | copy-start | bytes 18874372
  207.3 8.3 %copy-start.3 = (bf16[1,2048,768]{2,1,0:T(8,128)(2,1)S(1)}, bf16[1,2048,768]{2,1,0:T(8,128)(2,1)}, u32[]{:S(2)}) copy-start(bf16[1,2048,768]{2,1,0:T(8,128)(2,1)} %param.10) | copy-start | bytes 9437188
  215.5 8.0 %collective-permute-start = (f32[1536,768]{1,0:T(8,128)S(1)}, f32[1536,768]{1,0:T(8,128)S(1)}, u32[]{:S(2)}, u32[]{:S(2)}) collective-permute-start(f32[1536,768]{1,0:T(8,128)S(1)} %fusion.3), channel_id=1, source_target_pairs={{0,1},{1,0},{2,3},{3,2},{4,5},{5,4},{6,7},{7,6},{8,9},{9,8},{10,11... | collective-permute-start | bytes 14155784 | tf_op jit(solution)/shard_map/ppermute | solution.py:8
  220.8 9.5 %collective-permute-start.1 = (f32[1536,768]{1,0:T(8,128)S(1)}, f32[1536,768]{1,0:T(8,128)}, u32[]{:S(2)}, u32[]{:S(2)}) collective-permute-start(f32[1536,768]{1,0:T(8,128)S(1)} %fusion.1), channel_id=1, source_target_pairs={{0,1},{1,0},{2,3},{3,2},{4,5},{5,4},{6,7},{7,6},{8,9},{9,8},{10,11... | collective-permute-start | bytes 14155784 | tf_op jit(solution)/shard_map/ppermute | solution.py:8
  240.9 3.8 copy-start.2
  240.9 143.7 %all-to-all-start.2 = ((bf16[32,48,2048]{2,1,0:T(8,128)(2,1)}), bf16[32,48,2048]{2,1,0:T(8,128)(2,1)}, u32[]{:S(2)}, u32[]{:S(2)}) async-start(bf16[32,48,2048]{2,1,0:T(8,128)(2,1)} %bitcast.54), calls=%async_computation.2 | async-start | bytes 12582912 | tf_op jit(solution)/shard_map/all_to_all | solution.py:97
where the time goes:
time: 430 us; the launch traced here: 429 us
  waiting for transfers between devices  265 us (62%)
  local copies, waits for them, and re-layouts  96.1 us (22%)
  other arithmetic  25.3 us (6%)
  matrix products  24 us (6%)
  starting transfers between devices  17.8 us (4%)
    all_to_all x1, waiting for transfers between devices, on_device(): lax.all_to_all(outputs, ('node', 'ep'), split_axis=0, concat_axis=0, tile...  140 us
    all_to_all x1, waiting for transfers between devices, on_device(): lax.all_to_all(sent_quant, ('node', 'ep'), split_axis=0, concat_axis=0, t...  117 us
    mul x2, local copies, waits for them, and re-layouts, restore(): scaled = scaled * block_scales.astype(jnp.float32)[..., None]  22 us
    gather x1, local copies, waits for them, and re-layouts, on_device(): paired[flat_ids, :, positions_in].reshape(route_total, model_width)  16.2 us
    gather x1, local copies, waits for them, and re-layouts, on_device(): sent_quant = quant_rows[picked]  13.9 us
    reshape x1, local copies, waits for them, and re-layouts, on_device(): paired = returned.reshape(expert_count, 2, capacity, half_width)  12.7 us
    convert_element_type x1, other arithmetic, restore(): return (scaled.reshape(-1, row_width).astype(jnp.bfloat16), leading)  11.6 us
    dot_general x1, matrix products, expert_rows(): jnp.dot(hidden, down_half, preferred_element_type=jnp.float32)  10.6 us
  transfers between devices with their start and end apart: 5, of which 4 were waited for; matrix products, arithmetic and copies ran while one was open for 13% of the time, Pallas kernels for 0%

commit v1 on v0

--- a/solution.py
+++ b/solution.py
@@ -1,7 +1,13 @@
+import functools
+
 import jax
 import jax.numpy as jnp
 from jax import lax
+from jax.experimental import pallas as pl
+from jax.experimental.pallas import tpu as pltpu
 from jax.sharding import PartitionSpec as P
+
+LANES = 128
 
 
 def partner(array, axis, stride):
@@ -102,6 +108,337 @@
     return mixed.astype(jnp.bfloat16)
 
 
+def dense_kernel(
+    line_count,
+    tokens_ref,
+    ids_ref,
+    gates_ref,
+    gate_hbm,
+    up_hbm,
+    down_hbm,
+    out_ref,
+    x_buf,
+    part_buf,
+    diag_buf,
+    line_buf,
+    final_buf,
+    gate_w,
+    up_w,
+    down_w,
+    hidden,
+    w_local,
+    w_send,
+    w_recv,
+    z_send,
+    z_recv,
+    n_send,
+    n_recv,
+    d_send,
+    d_recv,
+    e_send,
+    e_recv,
+    f_send,
+    f_recv,
+    g_send,
+    g_recv,
+    h_send,
+    h_recv,
+):
+    node, ep = lax.axis_index("node"), lax.axis_index("ep")
+    core, z = lax.rem(ep, 2), ep // 2
+    expert = node * line_count + z
+    row_count, width = tokens_ref.shape
+    half_rows = row_count // 2
+    half_width = width // 2
+    route_count = ids_ref.shape[1]
+    expert_count = 4 * line_count
+    hidden_width = gate_w.shape[2]
+    batch = 2 * line_count * half_rows
+
+    x_peer = {"node": node + 1 - 2 * lax.rem(node, 2), "ep": ep}
+    y_peer = {"node": lax.rem(node + 2, 4), "ep": ep}
+    core_peer = {"node": node, "ep": ep + 1 - 2 * core}
+    sides = (x_peer, y_peer)
+
+    def z_peer(j):
+        return {"node": node, "ep": 2 * lax.rem(z + j, line_count) + core}
+
+    def slot(j):
+        return lax.rem(z + line_count - j, line_count)
+
+    def remote(src, dst, send, recv, device):
+        copy = pltpu.make_async_remote_copy(
+            src_ref=src,
+            dst_ref=dst,
+            send_sem=send,
+            recv_sem=recv,
+            device_id=device,
+            device_id_type=pl.DeviceIdType.MESH,
+        )
+        copy.start()
+        started.append(copy)
+        return copy
+
+    started = []
+    weights = ((gate_hbm, gate_w), (up_hbm, up_w), (down_hbm, down_w))
+    barrier = pltpu.get_barrier_semaphore()
+    peers = [x_peer, y_peer, core_peer] + [z_peer(j) for j in range(1, line_count)]
+    for peer in peers:
+        pl.semaphore_signal(barrier, inc=1, device_id=peer, device_id_type=pl.DeviceIdType.MESH)
+    local = []
+    for i, (hbm, held) in enumerate(weights):
+        copy = pltpu.make_async_copy(hbm.at[0], held.at[core], w_local.at[i])
+        copy.start()
+        local.append(copy)
+
+    def restore_block(b, carry):
+        columns = pl.ds(pl.multiple_of(b * LANES, LANES), LANES)
+        block = tokens_ref[:, columns].astype(jnp.float32)
+        largest = jnp.max(jnp.abs(block), axis=1, keepdims=True)
+        scale = ((largest + 1e-06) / 448.0).astype(jnp.bfloat16).astype(jnp.float32)
+        quantized = (block / scale).astype(jnp.bfloat16).astype(jnp.float32)
+        restored = (quantized * scale).astype(jnp.bfloat16)
+        x_buf[0, :, z, :, columns] = restored.reshape(2, half_rows, LANES)
+        return carry
+
+    lax.fori_loop(0, width // LANES, restore_block, 0, unroll=4)
+    lane = lax.broadcasted_iota(jnp.int32, (row_count, LANES), 1)
+    lane_expert = lax.rem(lane, expert_count)
+    table = jnp.zeros((row_count, LANES), jnp.float32)
+    for k in range(route_count):
+        table = table + jnp.where(ids_ref[:, k : k + 1] == lane_expert, gates_ref[:, k : k + 1], 0.0)
+    high = table.astype(jnp.bfloat16).astype(jnp.float32)
+    middle = (table - high).astype(jnp.bfloat16).astype(jnp.float32)
+    low = table - high - middle
+    pieces = jnp.where(
+        lane < expert_count,
+        high,
+        jnp.where(lane < 2 * expert_count, middle, jnp.where(lane < 3 * expert_count, low, 0.0)),
+    )
+    x_buf[0, :, z, :, width : width + LANES] = pieces.astype(jnp.bfloat16).reshape(
+        2, half_rows, LANES
+    )
+    pl.semaphore_wait(barrier, len(peers))
+
+    along = [
+        remote(x_buf.at[0, :, z], x_buf.at[0, :, z], z_send.at[j - 1], z_recv.at[j - 1], z_peer(j))
+        for j in range(1, line_count)
+    ]
+    across = []
+    for j in range(line_count):
+        if j > 0:
+            along[j - 1].wait_recv()
+        for s in range(2):
+            across.append(
+                remote(
+                    x_buf.at[0, :, slot(j)],
+                    x_buf.at[s + 1, :, slot(j)],
+                    n_send.at[s, j],
+                    n_recv.at[s, j],
+                    sides[s],
+                )
+            )
+        if j == 0:
+            moved = [
+                remote(hbm.at[0], held.at[core], w_send.at[i], w_recv.at[i], core_peer)
+                for i, (hbm, held) in enumerate(weights)
+            ]
+    for i in range(3):
+        local[i].wait()
+        moved[i].wait_recv()
+
+    def run_expert(group):
+        def hidden_tile(n, carry):
+            columns = pl.ds(pl.multiple_of(n * 256, 256), 256)
+            sums = []
+            for held in (gate_w, up_w):
+                total = None
+                for h in range(2):
+                    rows = x_buf[group, :, :, :, h * half_width : (h + 1) * half_width]
+                    term = jnp.dot(
+                        rows.reshape(batch, half_width),
+                        held[h, :, columns],
+                        preferred_element_type=jnp.float32,
+                    )
+                    total = term if total is None else total + term
+                sums.append(total)
+            gate_sum, up_sum = sums
+            act = gate_sum / (1.0 + jnp.exp(-gate_sum))
+            hidden[:, columns] = (act * up_sum).astype(jnp.bfloat16)
+            return carry
+
+        lax.fori_loop(0, hidden_width // 256, hidden_tile, 0)
+        spread = x_buf[group, :, :, :, width : width + LANES].reshape(batch, LANES)
+        lanes = lax.broadcasted_iota(jnp.int32, (batch, LANES), 1)
+        weight = jnp.sum(
+            jnp.where(lax.rem(lanes, expert_count) == expert, spread.astype(jnp.float32), 0.0),
+            axis=1,
+            keepdims=True,
+        )
+
+        for h in range(2):
+
+            def out_tile(n, carry):
+                columns = pl.ds(pl.multiple_of(n * 256, 256), 256)
+                result = jnp.dot(
+                    hidden[...], down_w[h, :, columns], preferred_element_type=jnp.float32
+                )
+                result = result.astype(jnp.bfloat16).astype(jnp.float32) * weight
+                target = pl.ds(pl.multiple_of(h * half_width + n * 256, 256), 256)
+                part_buf[group, :, :, :, target] = result.astype(jnp.bfloat16).reshape(
+                    2, line_count, half_rows, 256
+                )
+                return carry
+
+            lax.fori_loop(0, half_width // 256, out_tile, 0)
+
+    def add_into(target, terms):
+        def columns_of(n, carry):
+            columns = pl.ds(pl.multiple_of(n * 512, 512), 512)
+            index = (Ellipsis, columns)
+            total = terms[0][index].astype(jnp.float32)
+            for term in terms[1:]:
+                total = total + term[index].astype(jnp.float32)
+            target[index] = total.astype(jnp.bfloat16)
+            return carry
+
+        lax.fori_loop(0, width // 512, columns_of, 0)
+
+    run_expert(0)
+    corner = []
+    for j in range(line_count):
+        for s in range(2):
+            across[2 * j + s].wait_recv()
+            corner.append(
+                remote(
+                    x_buf.at[s + 1, s, slot(j)],
+                    x_buf.at[3, s, slot(j)],
+                    d_send.at[s, j],
+                    d_recv.at[s, j],
+                    sides[1 - s],
+                )
+            )
+    early = []
+    for s in range(2):
+        run_expert(s + 1)
+        early.append(
+            remote(
+                part_buf.at[s + 1, s], line_buf.at[s, s], e_send.at[s], e_recv.at[s], sides[s]
+            )
+        )
+    for copy in corner:
+        copy.wait_recv()
+    run_expert(3)
+    turned, late, home = {}, {}, []
+    order = list(range(1, line_count)) + [0]
+    for j in order:
+        for s in range(2):
+            turned[j, s] = remote(
+                part_buf.at[3, s, slot(j)],
+                diag_buf.at[s, slot(j)],
+                f_send.at[s, j],
+                f_recv.at[s, j],
+                sides[s],
+            )
+    for s in range(2):
+        early[s].wait_recv()
+    for j in order:
+        for s in range(2):
+            turned[j, s].wait_recv()
+            add_into(
+                part_buf.at[2 - s, s, slot(j)],
+                [part_buf.at[2 - s, s, slot(j)], diag_buf.at[s, slot(j)]],
+            )
+            late[j, s] = remote(
+                part_buf.at[2 - s, s, slot(j)],
+                line_buf.at[1 - s, s, slot(j)],
+                g_send.at[s, j],
+                g_recv.at[s, j],
+                sides[1 - s],
+            )
+    for j in order:
+        for s in range(2):
+            late[j, s].wait_recv()
+        if j > 0:
+            add_into(
+                part_buf.at[0, :, slot(j)],
+                [part_buf.at[0, :, slot(j)]] + [line_buf.at[s, :, slot(j)] for s in range(2)],
+            )
+            home.append(
+                remote(
+                    part_buf.at[0, :, slot(j)],
+                    final_buf.at[j - 1],
+                    h_send.at[j - 1],
+                    h_recv.at[j - 1],
+                    z_peer(line_count - j),
+                )
+            )
+    for copy in home:
+        copy.wait_recv()
+
+    def finish(n, carry):
+        columns = pl.ds(pl.multiple_of(n * 256, 256), 256)
+        total = part_buf[0, :, z, :, columns].astype(jnp.float32)
+        for s in range(2):
+            total = total + line_buf[s, :, z, :, columns].astype(jnp.float32)
+        for j in range(1, line_count):
+            total = total + final_buf[j - 1, :, :, columns].astype(jnp.float32)
+        out_ref[:, columns] = total.astype(jnp.bfloat16).reshape(row_count, 256)
+        return carry
+
+    lax.fori_loop(0, width // 256, finish, 0)
+    for copy in started:
+        copy.wait_send()
+
+
+def dense_on_device(tokens, expert_ids, gate_values, gate_weight, up_weight, down_weight):
+    row_count, model_width = tokens.shape
+    hidden_width = gate_weight.shape[2]
+    lines = lax.axis_size("ep") // 2
+    half_rows = row_count // 2
+    half_width = model_width // 2
+    vmem = pl.BlockSpec(memory_space=pltpu.VMEM)
+    anywhere = pl.BlockSpec(memory_space=pl.ANY)
+    dma = pltpu.SemaphoreType.DMA
+    return pl.pallas_call(
+        functools.partial(dense_kernel, lines),
+        out_shape=jax.ShapeDtypeStruct((row_count, model_width), jnp.bfloat16),
+        in_specs=[vmem] * 3 + [anywhere] * 3,
+        out_specs=vmem,
+        scratch_shapes=[
+            pltpu.VMEM((4, 2, lines, half_rows, model_width + LANES), jnp.bfloat16),
+            pltpu.VMEM((4, 2, lines, half_rows, model_width), jnp.bfloat16),
+            pltpu.VMEM((2, lines, half_rows, model_width), jnp.bfloat16),
+            pltpu.VMEM((2, 2, lines, half_rows, model_width), jnp.bfloat16),
+            pltpu.VMEM((lines - 1, 2, half_rows, model_width), jnp.bfloat16),
+            pltpu.VMEM((2, half_width, hidden_width), jnp.bfloat16),
+            pltpu.VMEM((2, half_width, hidden_width), jnp.bfloat16),
+            pltpu.VMEM((2, hidden_width, half_width), jnp.bfloat16),
+            pltpu.VMEM((2 * lines * half_rows, hidden_width), jnp.bfloat16),
+            dma((3,)),
+            dma((3,)),
+            dma((3,)),
+            dma((lines - 1,)),
+            dma((lines - 1,)),
+            dma((2, lines)),
+            dma((2, lines)),
+            dma((2, lines)),
+            dma((2, lines)),
+            dma((2,)),
+            dma((2,)),
+            dma((2, lines)),
+            dma((2, lines)),
+            dma((2, lines)),
+            dma((2, lines)),
+            dma((lines - 1,)),
+            dma((lines - 1,)),
+        ],
+        compiler_params=pltpu.CompilerParams(
+            collective_id=0, has_side_effects=True, vmem_limit_bytes=60 * 1024 * 1024
+        ),
+    )(tokens, expert_ids, gate_values, gate_weight, up_weight, down_weight)
+
+
 def solution(mesh):
     in_specs = (
         P(("groups", "node", "ep"), None),
@@ -112,6 +449,7 @@
         P(("node", "ep"), None, None),
     )
     out_specs = P(("groups", "node", "ep"), None)
+    few = mesh.shape["node"] == 4 and mesh.shape["ep"] <= 8
     return jax.shard_map(
-        on_device, mesh=mesh, in_specs=in_specs, out_specs=out_specs, check_vma=False
-    )
+        dense_on_device if few else on_device, mesh=mesh, in_specs=in_specs, out_specs=out_specs, check_vma=False
+    )

time: 430 us -> 194 us (0.45)
  waiting for transfers between devices: 265 us -> 0 us
  Pallas kernels: 0 us -> 189 us
  local copies, waits for them, and re-layouts: 96.1 us -> 4.62 us
  other arithmetic: 25.3 us -> 0 us
  matrix products: 24 us -> 0 us
  starting transfers between devices: 17.8 us -> 0 us
    all_to_all x3 -> x0, waiting for transfers between devices: 256 us -> none  [the longest x1 140 us: on_device(): lax.all_to_all(outputs, ('node', 'ep'), split_axis=0, concat_axis=0, tile...]
    pallas_call x0 -> x1, Pallas kernels: none -> 189 us  [dense_on_device(): pl.pallas_call(functools.partial(dense_kernel, lines), out_shape=jax.Shap...]
    gather x4 -> x0, local copies, waits for them, and re-layouts: 35.3 us -> none  [the longest x1 16.2 us: on_device(): paired[flat_ids, :, positions_in].reshape(route_total, model_width)]
    dot_general x3 -> x0, matrix products: 24 us -> none  [the longest x1 10.6 us: expert_rows(): jnp.dot(hidden, down_half, preferred_element_type=jnp.float32)]
    mul x2 -> x0, local copies, waits for them, and re-layouts: 22 us -> none  [restore(): scaled = scaled * block_scales.astype(jnp.float32)[..., None]]
    reshape x6 -> x0, local copies, waits for them, and re-layouts: 18 us -> none  [the longest x1 12.7 us: on_device(): paired = returned.reshape(expert_count, 2, capacity, half_width)]
    all_to_all x3 -> x0, starting transfers between devices: 17.2 us -> none  [the longest x1 7.3 us: on_device(): lax.all_to_all(sent_scales, ('node', 'ep'), split_axis=0, concat_axis=0,...]
    convert_element_type x3 -> x0, other arithmetic: 11.7 us -> none  [the longest x1 11.6 us: restore(): return (scaled.reshape(-1, row_width).astype(jnp.bfloat16), leading)]
  transfers between devices with their start and end apart: 5 -> 0, of which waited for: 4 -> 0; matrix products, arithmetic and copies ran while one was open for 13% -> 0% of each run, Pallas kernels for 0% -> 0%
where the time goes in v1:
time: 194 us
  Pallas kernels  189 us (97%)
  local copies, waits for them, and re-layouts  4.62 us (2%)
    pallas_call x1, Pallas kernels, dense_on_device(): pl.pallas_call(functools.partial(dense_kernel, lines), out_shape=jax.Shap...  189 us
    unnamed x3, local copies, waits for them, and re-layouts  4.62 us

profile of v1, /device:TPU:0, one launch (start us, length us, event | category | flops | bytes accessed | tf_op | source)
XLA Modules:
  0.0 193.9 jit_solution(18312853002627858572)
XLA Ops:
  0.0 1.4 copy.7.ids_ref
  1.4 1.4 copy.8.gates_ref
  2.8 189.3 %shard_map.64 = bf16[64,4096]{1,0:T(8,128)(2,1)} custom-call(bf16[64,4096]{1,0:T(8,128)(2,1)} %tokens_ref.1, s32[64,8]{1,0:T(8,128)} %copy.7.ids_ref, f32[64,8]{1,0:T(8,128)} %copy.8.gates_ref, bf16[1,2048,768]{2,1,0:T(8,128)(2,1)} %gate_hbm.1, bf16[1,2048,768]{2,1,0:T(8,128)(2,1)} %up_hbm.1, bf16[1,768,2048]{2,1,0:T(8,128)(2,1)} %down_hbm.1), custom_call_target="tpu_custom_call" | custom-call | tf_op jit(solution)/shard_map/pallas_call | solution.py:403
  192.1 1.9 copy.10
